TPU v7x, 512 devices: a whole 4x8x8 slice. The times are simulated.
512 devices in a mesh: dp: 64 (over y, z_lo, core), tp: 8 (over x, z_hi).
Axes of the slice: x: 4, y: 8, z: 8 (z_hi: 2, z_lo: 4; z = z_hi * 4 + z_lo), core: 2. Of those that a mesh axis runs over, the one named last changes fastest.
Arguments:
- hidden: bfloat16 [4096, 5120], P('dp'), may hold values from -6 to 6
- norm_gain: float32 [5120], replicated, may hold values from 0.1 to 1.9
- w_query: bfloat16 [5120, 4096], P(('dp', 'tp')), may hold values from -0.078125 to 0.078125
- w_key: bfloat16 [5120, 1024], P(('dp', 'tp')), may hold values from -0.078125 to 0.078125
- w_value: bfloat16 [5120, 1024], P(('dp', 'tp')), may hold values from -0.078125 to 0.078125
- w_out: bfloat16 [4096, 5120], P(None, ('dp', 'tp')), may hold values from -0.09375 to 0.09375
- key_cache: bfloat16 [4096, 8, 128, 128], P('dp', 'tp'), may hold values from -136 to 136
- value_cache: bfloat16 [4096, 8, 128, 128], P('dp', 'tp'), may hold values from -6 to 6
- lengths: int32 [4096], P('dp'), may hold values from 1 to 128
- positions: int32 [4096], P('dp'), may hold values from 0 to 8190
Outputs:
- mixed: bfloat16 [4096, 5120], P('dp', 'tp')
Inputs may be any that keep to these rules, and one draw needn't show every extreme that they name: `lengths`: slots at and beyond a row's length are not attended.
All inputs are finite; a program needn't handle non-finite values.
Results may differ from a plain program's by a relative error of at most 0.035.
The roundings to bfloat16 on the way count: a program that leaves them out, or rounds other values in their place, can miss the bound.
Values may be sent and summed in bfloat16 or wider, within the bound.
No kernel may reach another device: no remote copies, remote signals or barrier semaphores. Data moves between devices by JAX's collectives and lax.ppermute only.
A program may use at most 64 MiB of HBM per device.

v0:
```python
import math

import jax
import jax.numpy as jnp
from jax import lax
from jax.sharding import PartitionSpec as P

HD = 128


THETA = 1000000.0
EPS = 1e-06


def rotate(vectors, token_pos):
    half_dim = vectors.shape[-1] // 2
    inverse = jnp.exp(
        jnp.arange(half_dim).astype(jnp.float32) * (-2.0 * math.log(THETA) / vectors.shape[-1])
    )
    angles = token_pos.astype(jnp.float32)[:, None] * inverse[None, :]
    cosine = jnp.cos(angles)[:, None, :]
    sine = jnp.sin(angles)[:, None, :]
    front = vectors[..., :half_dim]
    back = vectors[..., half_dim:]
    return jnp.concatenate([front * cosine - back * sine, back * cosine + front * sine], axis=-1)


def rms_norm(values, gain):
    widened = values.astype(jnp.float32)
    factor = lax.rsqrt(jnp.mean(widened * widened, axis=1, keepdims=True) + EPS)
    return (widened * factor * gain).astype(jnp.bfloat16)


def heads_of(product, token_pos, q_width, kv_width, kv_heads):
    row_count = product.shape[0]
    queries = rotate(product[:, :q_width].reshape(row_count, q_width // HD, HD), token_pos).astype(
        jnp.bfloat16
    )
    queries = queries.reshape(row_count, kv_heads, q_width // HD // kv_heads, HD)
    keys_new = rotate(
        product[:, q_width : q_width + kv_width].reshape(row_count, kv_heads, HD), token_pos
    ).astype(jnp.bfloat16)
    values_new = (
        product[:, q_width + kv_width :].astype(jnp.bfloat16).reshape(row_count, kv_heads, HD)
    )
    return (queries, keys_new, values_new)


def attend(queries, key_cache, value_cache, lengths, new_keys, new_values):
    all_keys = jnp.concatenate([key_cache, new_keys], axis=2)
    all_values = jnp.concatenate([value_cache, new_values], axis=2)
    slots = jnp.arange(all_keys.shape[2])
    valid = (slots[None, :] < lengths[:, None]) | (slots[None, :] >= key_cache.shape[2])
    scores = jnp.einsum(
        "rhgd,rhld->rhgl", queries, all_keys, preferred_element_type=jnp.float32
    ) * queries.shape[-1] ** (-0.5)
    scores = jnp.where(valid[:, None, None, :], scores, -1e30)
    highest = jnp.max(scores, axis=-1, keepdims=True)
    weights = jnp.exp(scores - highest)
    weights = (weights / jnp.sum(weights, axis=-1, keepdims=True)).astype(jnp.bfloat16)
    summed = jnp.einsum("rhgl,rhld->rhgd", weights, all_values, preferred_element_type=jnp.float32)
    return summed.astype(jnp.bfloat16).reshape(queries.shape[0], -1)


def on_device(
    hidden, norm_gain, w_query, w_key, w_value, w_out, key_cache, value_cache, lengths, positions
):
    tp_count = lax.axis_size("tp")
    tp_rank = lax.axis_index("tp")
    model_width = hidden.shape[1]
    kv_local = key_cache.shape[1]
    q_width = w_query.shape[1] // tp_count
    kv_width = w_key.shape[1] // tp_count
    share_width = model_width // tp_count
    col_start = tp_rank * share_width
    query_part, key_part, value_part = (
        lax.all_to_all(w_query, "tp", split_axis=1, concat_axis=0, tiled=True),
        lax.all_to_all(w_key, "tp", split_axis=1, concat_axis=0, tiled=True),
        lax.all_to_all(w_value, "tp", split_axis=1, concat_axis=0, tiled=True),
    )
    joined_part = jnp.concatenate([query_part, key_part, value_part], axis=1)
    out_part = lax.all_to_all(w_out, "tp", split_axis=0, concat_axis=1, tiled=True)
    out_weight = lax.all_gather(out_part, "dp", axis=1, tiled=True)
    h_one = rms_norm(hidden, norm_gain)
    slice_weight = lax.all_gather(joined_part, "dp", axis=0, tiled=True)
    product_one = jnp.dot(h_one, slice_weight, preferred_element_type=jnp.float32)
    query_one, key_one, value_one = heads_of(product_one, positions, q_width, kv_width, kv_local)
    att_one = attend(
        query_one, key_cache, value_cache, lengths, key_one[:, :, None], value_one[:, :, None]
    )
    partial_one = jnp.dot(att_one, out_weight, preferred_element_type=jnp.float32)
    summed_whole = lax.psum(partial_one, "tp")
    middle = (hidden.astype(jnp.float32) + summed_whole).astype(jnp.bfloat16)
    h_two = rms_norm(middle, norm_gain)
    product_two = jnp.dot(h_two, slice_weight, preferred_element_type=jnp.float32)
    middle_share = lax.dynamic_slice_in_dim(middle, col_start, share_width, 1)
    query_two, key_two, value_two = heads_of(
        product_two, positions + 1, q_width, kv_width, kv_local
    )
    att_two = attend(
        query_two,
        key_cache,
        value_cache,
        lengths,
        jnp.stack([key_one, key_two], axis=2),
        jnp.stack([value_one, value_two], axis=2),
    )
    partial_two = jnp.dot(att_two, out_weight, preferred_element_type=jnp.float32)
    final_share = lax.psum_scatter(
        partial_two.astype(jnp.bfloat16), "tp", scatter_dimension=1, tiled=True
    ).astype(jnp.float32)
    return (middle_share.astype(jnp.float32) + final_share).astype(jnp.bfloat16)


def solution(mesh):
    return jax.shard_map(
        on_device,
        mesh=mesh,
        in_specs=(
            P("dp", None),
            P(),
            P(("dp", "tp"), None),
            P(("dp", "tp"), None),
            P(("dp", "tp"), None),
            P(None, ("dp", "tp")),
            P("dp", "tp", None, None),
            P("dp", "tp", None, None),
            P("dp"),
            P("dp"),
        ),
        out_specs=P("dp", "tp"),
        check_vma=False,
    )
```

profile of v0, /device:TPU:8, one launch (start us, length us, event | category | flops | bytes accessed | tf_op | source)
XLA Modules:
  0.0 575.7 jit_solution(18258966231094058734)
XLA Ops:
  6.5 0.0 copy-start
  6.5 0.0 copy-start.4
  6.5 0.0 copy-start.2
  6.5 0.0 copy-start.1
  6.5 0.8 copy.52
  7.4 0.6 copy.36
  8.0 12.7 %all-to-all-start.1 = ((bf16[10,8,128]{2,0,1:T(8,128)(2,1)}), bf16[10,8,128]{2,0,1:T(8,128)(2,1)S(1)}, u32[]{:S(2)}, u32[]{:S(2)}) async-start(bf16[10,8,128]{2,0,1:T(8,128)(2,1)} %copy.36), calls=%async_computation.1 | async-start | bytes 65536 | tf_op jit(solution)/shard_map/all_to_all | solution.py:78
  20.7 0.8 copy.53
  21.5 0.6 copy.37
  22.1 8.8 %all-to-all-done.1 = bf16[10,8,128]{2,0,1:T(8,128)(2,1)S(1)} async-done(((bf16[10,8,128]{2,0,1:T(8,128)(2,1)}), bf16[10,8,128]{2,0,1:T(8,128)(2,1)S(1)}, u32[]{:S(2)}, u32[]{:S(2)}) %all-to-all-start.1) | async-done | bytes 20512 | tf_op jit(solution)/shard_map/all_to_all | solution.py:78
  30.9 3.3 all-to-all-start.2
  34.3 0.9 copy.51
  35.2 0.7 copy.35
  35.9 8.4 %all-to-all-done.2 = bf16[10,8,128]{2,0,1:T(8,128)(2,1)S(1)} async-done(((bf16[10,8,128]{2,0,1:T(8,128)(2,1)}), bf16[10,8,128]{2,0,1:T(8,128)(2,1)S(1)}, u32[]{:S(2)}, u32[]{:S(2)}) %all-to-all-start.2) | async-done | bytes 20512 | tf_op jit(solution)/shard_map/all_to_all | solution.py:79
  44.3 3.4 all-to-all-start
  47.7 0.0 all-gather.3.cloned.1.call-start
  47.8 10.4 %all-to-all-done = bf16[10,8,512]{2,0,1:T(8,128)(2,1)S(1)} async-done(((bf16[10,8,512]{2,0,1:T(8,128)(2,1)}), bf16[10,8,512]{2,0,1:T(8,128)(2,1)S(1)}, u32[]{:S(2)}, u32[]{:S(2)}) %all-to-all-start) | async-done | bytes 81952 | tf_op jit(solution)/shard_map/all_to_all | solution.py:77
  58.3 0.7 pad_maximum_fusion
  59.0 0.0 all-gather.3.cloned.1.call-update
  59.0 0.0 all-gather.5.cloned.1.call-start
  59.0 0.9 copy.55
  60.0 13.0 %all_to_all.76 = bf16[8,512,10]{1,2,0:T(8,128)(2,1)S(1)} all-to-all(bf16[8,512,10]{1,2,0:T(8,128)(2,1)S(1)} %copy.42), channel_id=1, replica_groups=mesh['dp'=64,'tp'=8] {'tp'}, dimensions={0} | all-to-all | bytes 163840 | tf_op jit(solution)/shard_map/all_to_all | solution.py:82
  73.0 0.7 all_to_all.71
  73.7 0.0 all-gather.5.cloned.1.call-update
  73.7 0.0 all-reduce.2.cloned.1.call-start
  73.8 0.0 copy-done
  73.8 0.2 fusion.21
  74.1 0.0 copy-done.4
  74.1 0.0 copy-done.2
  74.1 0.1 fusion.56
  74.2 0.3 multiply_cosine_fusion.1
  74.5 0.0 copy-start.3
  74.5 105.5 %all-gather.3.cloned.1.call-done = bf16[5120,768]{1,0:T(8,128)(2,1)} async-done(((bf16[80,768]{1,0:T(8,128)(2,1)}), bf16[5120,768]{1,0:T(8,128)(2,1)}) %all-gather.3.cloned.1.call-update) | async-done | bytes 7864336 | tf_op jit(solution)/shard_map/all_gather | solution.py:85
  180.0 0.0 copy-done.1
  180.0 4.8 fusion.35
  184.8 0.2 fusion.79
  185.0 0.1 pad_maximum_fusion.1
  185.2 0.2 subtract_convert_fusion.1
  185.4 0.0 copy-done.3
  185.4 2.1 fusion.94
  187.5 2.4 fusion.33
  189.9 112.0 %all-gather.5.cloned.1.call-done = bf16[512,5120]{0,1:T(8,128)(2,1)} async-done(((bf16[512,80]{0,1:T(8,128)(2,1)}), bf16[512,5120]{0,1:T(8,128)(2,1)}) %all-gather.5.cloned.1.call-update) | async-done | bytes 5242896 | tf_op jit(solution)/shard_map/all_gather | solution.py:83
  302.0 5.2 fusion.47
  307.2 0.0 all-reduce.2.cloned.1.call-update
  307.2 0.0 reduce-scatter.4.cloned.1.call-start
  307.3 0.1 fusion.57
  307.4 147.7 %all-reduce.2.cloned.1.call-done = f32[64,5120]{1,0:T(8,128)} async-done(((f32[64,5120]{1,0:T(8,128)}), f32[64,5120]{1,0:T(8,128)}) %all-reduce.2.cloned.1.call-update) | async-done | bytes 1310736 | tf_op jit(solution)/shard_map/psum | solution.py:92
  455.0 1.6 fusion.18
  456.7 4.8 fusion.37
  461.6 0.2 fusion.81
  461.8 0.1 pad_maximum_fusion.2
  461.9 0.2 subtract_convert_fusion
  462.1 3.1 fusion.97
  465.1 2.3 fusion.32
  467.5 4.2 convolution_convert_fusion
  471.7 1.4 copy.49
  473.1 0.0 reduce-scatter.4.cloned.1.call-update
  473.1 94.4 %reduce-scatter.4.cloned.1.call-done = bf16[640,64]{1,0:T(8,128)(2,1)} async-done(((bf16[5120,64]{1,0:T(8,128)(2,1)}), bf16[640,64]{1,0:T(8,128)(2,1)}) %reduce-scatter.4.cloned.1.call-update) | async-done | bytes 81936
  567.5 1.0 copy.50
  568.5 0.7 add_convert_fusion
  (26 shorter events, 0.4 us)
Async XLA Ops:
  6.5 67.3 %copy-start = (bf16[64,5120]{1,0:T(8,128)(2,1)S(1)}, bf16[64,5120]{1,0:T(8,128)(2,1)}, u32[]{:S(2)}) copy-start(bf16[64,5120]{1,0:T(8,128)(2,1)} %param.10) | copy-start | bytes 1966084
  6.5 67.5 %copy-start.4 = (s32[64]{0:T(128)S(1)}, s32[64]{0:T(128)}, u32[]{:S(2)}) copy-start(s32[64]{0:T(128)} %param.19) | copy-start | bytes 772
  6.5 67.6 %copy-start.2 = (s32[64]{0:T(128)S(1)}, s32[64]{0:T(128)}, u32[]{:S(2)}) copy-start(s32[64]{0:T(128)} %param.18) | copy-start | bytes 772
  6.5 173.4 %copy-start.1 = (f32[5120]{0:T(1024)S(1)}, f32[5120]{0:T(1024)}, u32[]{:S(2)}) copy-start(f32[5120]{0:T(1024)} %param.11) | copy-start | bytes 61444
  8.0 22.9 %all-to-all-start.1 = ((bf16[10,8,128]{2,0,1:T(8,128)(2,1)}), bf16[10,8,128]{2,0,1:T(8,128)(2,1)S(1)}, u32[]{:S(2)}, u32[]{:S(2)}) async-start(bf16[10,8,128]{2,0,1:T(8,128)(2,1)} %copy.36), calls=%async_computation.1 | async-start | bytes 65536 | tf_op jit(solution)/shard_map/all_to_all | solution.py:78
  30.9 13.4 %all-to-all-start.2 = ((bf16[10,8,128]{2,0,1:T(8,128)(2,1)}), bf16[10,8,128]{2,0,1:T(8,128)(2,1)S(1)}, u32[]{:S(2)}, u32[]{:S(2)}) async-start(bf16[10,8,128]{2,0,1:T(8,128)(2,1)} %copy.37), calls=%async_computation.2 | async-start | bytes 65536 | tf_op jit(solution)/shard_map/all_to_all | solution.py:79
  44.3 13.9 %all-to-all-start = ((bf16[10,8,512]{2,0,1:T(8,128)(2,1)}), bf16[10,8,512]{2,0,1:T(8,128)(2,1)S(1)}, u32[]{:S(2)}, u32[]{:S(2)}) async-start(bf16[10,8,512]{2,0,1:T(8,128)(2,1)} %copy.35), calls=%async_computation | async-start | bytes 262144 | tf_op jit(solution)/shard_map/all_to_all | solution.py:77
  47.7 132.3 %all-gather.3.cloned.1.call-start = ((), (), s32[]{:S(2)}) async-start(), calls=%async_computation.5 | async-start | bytes 7987200 | tf_op jit(solution)/shard_map/all_gather | solution.py:85
  59.0 243.0 %all-gather.5.cloned.1.call-start = ((), (), s32[]{:S(2)}) async-start(), calls=%async_computation.6 | async-start | bytes 5324800 | tf_op jit(solution)/shard_map/all_gather | solution.py:83
  73.7 381.3 %all-reduce.2.cloned.1.call-start = ((), (), s32[]{:S(2)}) async-start(), calls=%async_computation.7 | async-start | bytes 2621440 | tf_op jit(solution)/shard_map/psum | solution.py:92
  74.5 110.9 %copy-start.3 = (bf16[64,1,128,128]{3,2,1,0:T(8,128)(2,1)S(1)}, bf16[64,1,128,128]{3,2,1,0:T(8,128)(2,1)}, u32[]{:S(2)}) copy-start(bf16[64,1,128,128]{3,2,1,0:T(8,128)(2,1)} %param.16) | copy-start | bytes 6291460
  307.2 260.2 %reduce-scatter.4.cloned.1.call-start = ((), (), s32[]{:S(2)}) async-start(), calls=%async_computation.8 | async-start | bytes 1474560
Sparse Core Ops, SparseCore 0:
  59.1 120.8 all-gather.2
  182.1 119.7 all-gather.4
  307.4 147.6 all-reduce.1
  473.2 94.1 reduce-scatter.3
where the time goes:
time: 576 us
  waiting for transfers between devices  487 us (85%)
  matrix products  28.9 us (5%)
  starting transfers between devices  19.6 us (3%)
  between operations  13.4 us (2%)
  blocking collectives  13 us (2%)
  local copies, waits for them, and re-layouts  8.92 us (2%)
    psum x1, waiting for transfers between devices, on_device(): summed_whole = lax.psum(partial_one, 'tp')  148 us
    all_gather x1, waiting for transfers between devices, on_device(): out_weight = lax.all_gather(out_part, 'dp', axis=1, tiled=True)  112 us
    all_gather x1, waiting for transfers between devices, on_device(): slice_weight = lax.all_gather(joined_part, 'dp', axis=0, tiled=True)  105 us
    unnamed x5, waiting for transfers between devices  94.4 us
    all_to_all x1, blocking collectives, on_device(): lax.all_to_all(w_out, 'tp', split_axis=0, concat_axis=1, tiled=True)  13 us
    all_to_all x1, starting transfers between devices, on_device(): lax.all_to_all(w_key, 'tp', split_axis=1, concat_axis=0, tiled=True)  12.7 us
  transfers between devices with their start and end apart: 7, of which 7 were waited for; matrix products, arithmetic and copies ran while one was open for 3% of the time, Pallas kernels for 0%

commit v1 on v0

--- a/solution.py
+++ b/solution.py
@@ -67,33 +67,53 @@
 ):
     tp_count = lax.axis_size("tp")
     tp_rank = lax.axis_index("tp")
-    model_width = hidden.shape[1]
+    rows, model_width = hidden.shape
     kv_local = key_cache.shape[1]
     q_width = w_query.shape[1] // tp_count
     kv_width = w_key.shape[1] // tp_count
     share_width = model_width // tp_count
     col_start = tp_rank * share_width
-    query_part, key_part, value_part = (
-        lax.all_to_all(w_query, "tp", split_axis=1, concat_axis=0, tiled=True),
-        lax.all_to_all(w_key, "tp", split_axis=1, concat_axis=0, tiled=True),
-        lax.all_to_all(w_value, "tp", split_axis=1, concat_axis=0, tiled=True),
+
+    def by_slice(flat):
+        return flat.reshape(flat.shape[0], tp_count, -1).transpose(1, 0, 2)
+
+    packed = jnp.concatenate(
+        [by_slice(w_query), by_slice(w_key), by_slice(w_value), by_slice(w_out.T)], axis=2
     )
-    joined_part = jnp.concatenate([query_part, key_part, value_part], axis=1)
-    out_part = lax.all_to_all(w_out, "tp", split_axis=0, concat_axis=1, tiled=True)
-    out_weight = lax.all_gather(out_part, "dp", axis=1, tiled=True)
+    packed = lax.all_to_all(packed, "tp", split_axis=0, concat_axis=0, tiled=True)
+    packed = packed.reshape(-1, packed.shape[2])
+    gathered = lax.all_gather(packed, "dp", axis=0, tiled=True)
+    slice_weight = gathered[:, : q_width + 2 * kv_width]
+    out_weight = gathered[:, q_width + 2 * kv_width :].T
+
+    def sum_over_heads(partial):
+        blocks = partial.astype(jnp.bfloat16).reshape(rows, tp_count, share_width)
+        blocks = lax.all_to_all(
+            blocks.transpose(1, 0, 2), "tp", split_axis=0, concat_axis=0, tiled=True
+        )
+        return jnp.sum(blocks.astype(jnp.float32), axis=0)
+
+    hidden_share = lax.dynamic_slice_in_dim(hidden, col_start, share_width, 1)
     h_one = rms_norm(hidden, norm_gain)
-    slice_weight = lax.all_gather(joined_part, "dp", axis=0, tiled=True)
     product_one = jnp.dot(h_one, slice_weight, preferred_element_type=jnp.float32)
     query_one, key_one, value_one = heads_of(product_one, positions, q_width, kv_width, kv_local)
     att_one = attend(
         query_one, key_cache, value_cache, lengths, key_one[:, :, None], value_one[:, :, None]
     )
     partial_one = jnp.dot(att_one, out_weight, preferred_element_type=jnp.float32)
-    summed_whole = lax.psum(partial_one, "tp")
-    middle = (hidden.astype(jnp.float32) + summed_whole).astype(jnp.bfloat16)
+    middle_share = (hidden_share.astype(jnp.float32) + sum_over_heads(partial_one)).astype(
+        jnp.bfloat16
+    )
+    middle = lax.all_to_all(
+        jnp.broadcast_to(middle_share[None], (tp_count, rows, share_width)),
+        "tp",
+        split_axis=0,
+        concat_axis=0,
+        tiled=True,
+    )
+    middle = middle.transpose(1, 0, 2).reshape(rows, model_width)
     h_two = rms_norm(middle, norm_gain)
     product_two = jnp.dot(h_two, slice_weight, preferred_element_type=jnp.float32)
-    middle_share = lax.dynamic_slice_in_dim(middle, col_start, share_width, 1)
     query_two, key_two, value_two = heads_of(
         product_two, positions + 1, q_width, kv_width, kv_local
     )
@@ -106,9 +126,7 @@
         jnp.stack([value_one, value_two], axis=2),
     )
     partial_two = jnp.dot(att_two, out_weight, preferred_element_type=jnp.float32)
-    final_share = lax.psum_scatter(
-        partial_two.astype(jnp.bfloat16), "tp", scatter_dimension=1, tiled=True
-    ).astype(jnp.float32)
+    final_share = sum_over_heads(partial_two)
     return (middle_share.astype(jnp.float32) + final_share).astype(jnp.bfloat16)
 
 

time: 576 us -> 277 us (0.48)
  the two profiles are of different devices: /device:TPU:8 before, /device:TPU:73 now
where the time goes in v1:
time: 277 us; the launch traced here: 276 us
  waiting for transfers between devices  168 us (61%)
  blocking collectives  46.2 us (17%)
  matrix products  25.7 us (9%)
  between operations  13.7 us (5%)
  starting transfers between devices  12.3 us (4%)
  local copies, waits for them, and re-layouts  6.66 us (2%)
  other arithmetic  2.88 us (1%)
    all_gather x1, waiting for transfers between devices, on_device(): gathered = lax.all_gather(packed, 'dp', axis=0, tiled=True)  128 us
    all_to_all x1, blocking collectives, on_device(): lax.all_to_all(packed, 'tp', split_axis=0, concat_axis=0, tiled=True)  25.2 us
    all_to_all x1, waiting for transfers between devices, sum_over_heads(): lax.all_to_all(blocks.transpose(1, 0, 2), 'tp', split_axis=0, concat_axis...  22.5 us
    all_to_all x1, blocking collectives, sum_over_heads(): lax.all_to_all(blocks.transpose(1, 0, 2), 'tp', split_axis=0, concat_axis...  21 us
    all_to_all x1, waiting for transfers between devices, on_device(): lax.all_to_all(jnp.broadcast_to(middle_share[None], (tp_count, rows, shar...  17.7 us
    all_to_all x1, starting transfers between devices, sum_over_heads(): lax.all_to_all(blocks.transpose(1, 0, 2), 'tp', split_axis=0, concat_axis...  8.76 us
  transfers between devices with their start and end apart: 3, of which 3 were waited for; matrix products, arithmetic and copies ran while one was open for 0% of the time, Pallas kernels for 0%

profile of v1, /device:TPU:73, one launch (start us, length us, event | category | flops | bytes accessed | tf_op | source)
XLA Modules:
  0.0 275.9 jit_solution(4402344040759590826)
XLA Ops:
  6.5 0.0 copy-start
  6.5 0.0 copy-start.5
  6.5 0.0 copy-start.1
  6.5 0.0 all-gather.2.cloned.1.call-start
  6.5 0.0 copy-start.4
  6.5 0.8 copy.72
  7.4 0.8 copy.73
  8.2 0.9 copy.71
  9.1 0.9 copy.74
  10.1 0.1 copy_bitcast_fusion
  10.2 25.2 %all_to_all.20 = bf16[8,10,1280]{2,1,0:T(8,128)(2,1)S(1)} all-to-all(bf16[8,10,1280]{2,1,0:T(8,128)(2,1)S(1)} %pad_maximum_fusion), channel_id=1, replica_groups=mesh['dp'=64,'tp'=8] {'tp'}, dimensions={0} | all-to-all | bytes 409600 | tf_op jit(solution)/shard_map/all_to_all | solution.py:83
  35.4 0.8 reshape.474
  36.2 0.0 all-gather.2.cloned.1.call-update
  36.3 0.0 copy-done
  36.3 0.2 fusion.24
  36.5 0.0 copy-done.5
  36.5 0.0 copy-done.1
  36.5 0.1 fusion.55
  36.6 0.3 multiply_cosine_fusion.1
  36.9 0.0 copy-start.2
  37.0 128.3 %all-gather.2.cloned.1.call-done = bf16[5120,1280]{1,0:T(8,128)(2,1)} async-done(((bf16[80,1280]{1,0:T(8,128)(2,1)}), bf16[5120,1280]{1,0:T(8,128)(2,1)}) %all-gather.2.cloned.1.call-update) | async-done | bytes 13107216 | tf_op jit(solution)/shard_map/all_gather | solution.py:85
  165.2 0.0 copy-done.4
  165.2 4.8 %fusion.4 = f32[64,768]{1,0:T(8,128)S(1)} fusion(bf16[5120,1280]{1,0:T(8,128)(2,1)} %all-gather.2.cloned.1.call-done, bf16[64,5120]{1,0:T(8,128)(2,1)S(1)} %copy-done, f32[5120]{0:T(1024)S(1)} %copy-done.4, f32[64]{0:T(128)S(1)} %add_rsqrt_fusion.1), kind=kOutput, calls=%fused_computation.4 | convolution fusion | flops 504627200 | bytes 8737024 | tf_op jit(solution)/shard_map/dot_general | solution.py:98
  170.1 0.2 fusion.78
  170.3 0.1 pad_maximum_fusion.1
  170.4 0.2 subtract_convert_fusion.1
  170.6 0.0 copy-done.2
  170.6 1.5 fusion.92
  172.1 2.3 fusion.36
  174.4 4.2 %convolution_convert_fusion.1 = bf16[64,5120]{1,0:T(8,128)(2,1)S(1)} fusion(bf16[5120,1280]{1,0:T(8,128)(2,1)} %all-gather.2.cloned.1.call-done, bf16[8,8,4,128]{3,2,1,0:T(4,128)(2,1)S(1)} %bitcast.116), kind=kOutput, calls=%fused_computation.7 | convolution fusion | flops 335872000 | bytes 5963776 | tf_op jit(solution)/shard_map/dot_general | solution.py:103
  178.6 1.0 copy.92
  179.6 8.8 %all-to-all-start.1 = ((bf16[8,64,640]{2,1,0:T(8,128)(2,1)}), bf16[8,64,640]{2,1,0:T(8,128)(2,1)S(1)}, u32[]{:S(2)}, u32[]{:S(2)}) async-start(bf16[8,64,640]{2,1,0:T(8,128)(2,1)} %bitcast.98), calls=%async_computation.1 | async-start | bytes 1310720 | tf_op jit(solution)/shard_map/all_to_all | solution.py:91
  188.3 22.5 %all-to-all-done.1 = bf16[8,64,640]{2,1,0:T(8,128)(2,1)S(1)} async-done(((bf16[8,64,640]{2,1,0:T(8,128)(2,1)}), bf16[8,64,640]{2,1,0:T(8,128)(2,1)S(1)}, u32[]{:S(2)}, u32[]{:S(2)}) %all-to-all-start.1) | async-done | bytes 655392 | tf_op jit(solution)/shard_map/all_to_all | solution.py:91
  210.8 0.1 convert_reduce_fusion.1
  211.0 0.9 broadcast_in_dim.25
  211.9 3.5 %all-to-all-start.2 = ((bf16[8,64,640]{2,1,0:T(8,128)(2,1)}), bf16[8,64,640]{2,1,0:T(8,128)(2,1)S(1)}, u32[]{:S(2)}, u32[]{:S(2)}) async-start(bf16[8,64,640]{2,1,0:T(8,128)(2,1)} %broadcast_in_dim.25), calls=%async_computation.2 | async-start | bytes 1310720 | tf_op jit(solution)/shard_map/all_to_all | solution.py:107
  215.5 0.1 fusion.56
  215.5 17.7 %all-to-all-done.2 = bf16[8,64,640]{2,1,0:T(8,128)(2,1)S(1)} async-done(((bf16[8,64,640]{2,1,0:T(8,128)(2,1)}), bf16[8,64,640]{2,1,0:T(8,128)(2,1)S(1)}, u32[]{:S(2)}, u32[]{:S(2)}) %all-to-all-start.2) | async-done | bytes 655392 | tf_op jit(solution)/shard_map/all_to_all | solution.py:107
  233.2 0.2 fusion.27
  233.5 0.1 convert_bitcast_fusion
  233.6 0.1 copy.70
  233.7 0.0 copy-start.3
  233.7 4.9 %fusion.2 = f32[64,768]{1,0:T(8,128)S(1)} fusion(bf16[5120,1280]{1,0:T(8,128)(2,1)} %all-gather.2.cloned.1.call-done, f32[64,5120]{1,0:T(8,128)S(1)} %bitcast.100, f32[64]{0:T(128)S(1)} %add_rsqrt_fusion, f32[5120]{0:T(1024)S(1)} %copy-done.4), kind=kOutput, calls=%fused_computation.2 | convolution fusion | flops 504299520 | bytes 9392384 | tf_op jit(solution)/shard_map/dot_general | solution.py:116
  238.7 0.2 fusion.80
  238.9 0.1 pad_maximum_fusion.2
  239.1 0.2 subtract_convert_fusion
  239.2 0.0 copy-done.3
  239.2 1.5 fusion.95
  240.7 2.4 fusion.35
  243.1 4.2 %convolution_convert_fusion = bf16[64,5120]{1,0:T(8,128)(2,1)S(1)} fusion(bf16[5120,1280]{1,0:T(8,128)(2,1)} %all-gather.2.cloned.1.call-done, bf16[8,8,4,128]{3,2,1,0:T(4,128)(2,1)S(1)} %bitcast.115), kind=kOutput, calls=%fused_computation.6 | convolution fusion | flops 335872000 | bytes 5963776 | tf_op jit(solution)/shard_map/dot_general | solution.py:128
  247.2 0.1 copy.91
  247.3 21.0 %all_to_all.21 = bf16[8,64,640]{2,1,0:T(8,128)(2,1)S(1)} all-to-all(bf16[8,64,640]{2,1,0:T(8,128)(2,1)S(1)} %bitcast.99), channel_id=1, replica_groups=mesh['dp'=64,'tp'=8] {'tp'}, dimensions={0} | all-to-all | bytes 1310720 | tf_op jit(solution)/shard_map/all_to_all | solution.py:91
  268.3 0.1 convert_reduce_fusion
  268.4 0.7 add_convert_fusion
  (25 shorter events, 0.4 us)
Async XLA Ops:
  6.5 29.7 %copy-start = (bf16[64,5120]{1,0:T(8,128)(2,1)S(1)}, bf16[64,5120]{1,0:T(8,128)(2,1)}, u32[]{:S(2)}) copy-start(bf16[64,5120]{1,0:T(8,128)(2,1)} %param.10) | copy-start | bytes 1966084
  6.5 30.0 %copy-start.5 = (s32[64]{0:T(128)S(1)}, s32[64]{0:T(128)}, u32[]{:S(2)}) copy-start(s32[64]{0:T(128)} %param.19) | copy-start | bytes 772
  6.5 30.0 %copy-start.1 = (s32[64]{0:T(128)S(1)}, s32[64]{0:T(128)}, u32[]{:S(2)}) copy-start(s32[64]{0:T(128)} %param.18) | copy-start | bytes 772
  6.5 158.7 %all-gather.2.cloned.1.call-start = ((), (), s32[]{:S(2)}) async-start(), calls=%async_computation.4 | async-start | bytes 13312000 | tf_op jit(solution)/shard_map/all_gather | solution.py:85
  6.5 158.7 %copy-start.4 = (f32[5120]{0:T(1024)S(1)}, f32[5120]{0:T(1024)}, u32[]{:S(2)}) copy-start(f32[5120]{0:T(1024)} %param.11) | copy-start | bytes 61444
  36.9 133.7 %copy-start.2 = (bf16[64,1,128,128]{3,2,1,0:T(8,128)(2,1)S(1)}, bf16[64,1,128,128]{3,2,1,0:T(8,128)(2,1)}, u32[]{:S(2)}) copy-start(bf16[64,1,128,128]{3,2,1,0:T(8,128)(2,1)} %param.16) | copy-start | bytes 6291460
  179.6 31.3 %all-to-all-start.1 = ((bf16[8,64,640]{2,1,0:T(8,128)(2,1)}), bf16[8,64,640]{2,1,0:T(8,128)(2,1)S(1)}, u32[]{:S(2)}, u32[]{:S(2)}) async-start(bf16[8,64,640]{2,1,0:T(8,128)(2,1)} %bitcast.98), calls=%async_computation.1 | async-start | bytes 1310720 | tf_op jit(solution)/shard_map/all_to_all | solution.py:91
  211.9 21.3 %all-to-all-start.2 = ((bf16[8,64,640]{2,1,0:T(8,128)(2,1)}), bf16[8,64,640]{2,1,0:T(8,128)(2,1)S(1)}, u32[]{:S(2)}, u32[]{:S(2)}) async-start(bf16[8,64,640]{2,1,0:T(8,128)(2,1)} %broadcast_in_dim.25), calls=%async_computation.2 | async-start | bytes 1310720 | tf_op jit(solution)/shard_map/all_to_all | solution.py:107
  233.7 5.6 %copy-start.3 = (bf16[64,1,128,128]{3,2,1,0:T(8,128)(2,1)S(1)}, bf16[64,1,128,128]{3,2,1,0:T(8,128)(2,1)}, u32[]{:S(2)}) copy-start(bf16[64,1,128,128]{3,2,1,0:T(8,128)(2,1)} %param.16) | copy-start | bytes 6291460
Sparse Core Ops, SparseCore 0:
  36.4 128.8 all-gather.1
